TPU v7x, 32 devices: a whole 2x2x4 slice. The times are simulated.
32 devices in a mesh: grp: 4 (over y, x), row: 8 (over z, core).
Axes of the slice: x: 2, y: 2, z: 4, core: 2. Of those that a mesh axis runs over, the one named last changes fastest.
Arguments:
- t_start: bfloat16 [8192, 512], P(('row', 'grp')), may hold values from -6 to 6
- h_blocks: bfloat16 [64, 4, 8, 128, 128], P('row', 'grp'), may hold values from -0.09375 to 0.09375
- h_cols: int32 [64, 4, 8], P('row', 'grp'), may hold values from 0 to 63, as said below
- t_cols: int32 [64, 3], P(('row', 'grp')), may hold values from 0 to 3, as said below
Outputs:
- t_before: bfloat16 [8192, 512], P(('row', 'grp'))
- t_last: bfloat16 [8192, 512], P(('row', 'grp'))
Inputs may be any that keep to these rules, and one draw needn't show every extreme that they name: The 8 entries of h_cols[b, g] differ, and each names a block row c with (c // 2) % 4 == g. `t_cols`: the 3 entries of a row differ.
All inputs are finite; a program needn't handle non-finite values.
Results may differ from a plain program's by a relative error of at most 0.025.
Values may be sent and summed in bfloat16 or wider, within the bound.
A program may use at most 64 MiB of HBM per device.

v0:
```python
import jax
import jax.numpy as jnp
from jax import lax
from jax.sharding import PartitionSpec as P

BS = 128
STEPS = 3


def per_device(t_start, h_blocks, h_cols, t_cols):
    groups = lax.axis_size("grp")
    rows_here = t_start.shape[0] // BS
    width = t_start.shape[1]
    col_blocks = width // BS
    blocks = h_blocks[:, 0]
    columns = h_cols[:, 0]
    local_index = columns // (groups * rows_here) * rows_here + columns % rows_here
    block_ids = jnp.arange(col_blocks, dtype=jnp.int32)
    kept = jnp.any(t_cols[:, :, None] == block_ids[None, None, :], axis=1)
    keep = kept.astype(jnp.float32)[:, None, :, None]

    def masked(values):
        shaped = values.reshape(rows_here, BS, col_blocks, BS) * keep
        return shaped.reshape(rows_here * BS, width)

    def apply_slab(slab):
        gathered = lax.all_gather(slab, "row", axis=0, tiled=True).reshape(-1, BS, width)
        picked = gathered[local_index]
        result = jnp.einsum("rsij,rsjm->rim", blocks, picked, preferred_element_type=jnp.float32)
        summed = lax.psum_scatter(
            result.astype(jnp.bfloat16).astype(jnp.float32).astype(jnp.bfloat16),
            "grp",
            scatter_dimension=0,
            tiled=True,
        ).astype(jnp.float32)
        return summed.reshape(rows_here * BS, width)

    first = masked(apply_slab(t_start)).astype(jnp.bfloat16)
    before, latest = (t_start, first)
    for step in range(STEPS - 1):
        summed = apply_slab(latest)
        after = masked(2.0 * summed - before.astype(jnp.float32)).astype(jnp.bfloat16)
        before, latest = (latest, after)
    return (before, latest)


def solution(mesh):
    placed = (
        P(("row", "grp"), None),
        P("row", "grp", None, None, None),
        P("row", "grp", None),
        P(("row", "grp"), None),
    )
    return jax.shard_map(
        per_device,
        mesh=mesh,
        in_specs=placed,
        out_specs=(P(("row", "grp"), None), P(("row", "grp"), None)),
        check_vma=False,
    )
```

profile of v0, /device:TPU:0, one launch (start us, length us, event | category | flops | bytes accessed | tf_op | source)
XLA Modules:
  0.0 241.7 jit_solution(15152453608066359497)
XLA Ops:
  7.2 0.0 copy-start
  7.2 0.0 all-gather.4.cloned.1.call-start
  7.2 0.7 all-gather.4.cloned.1.call-update
  7.9 0.0 reduce-scatter.4.cloned.1.call-start
  8.0 0.7 compare_select_fusion
  8.7 0.1 reshape.162
  8.8 32.7 %all-gather.4.cloned.1.call-done = bf16[2048,512]{1,0:T(8,128)(2,1)} async-done(((bf16[256,512]{1,0:T(8,128)(2,1)}), bf16[2048,512]{1,0:T(8,128)(2,1)}) %all-gather.4.cloned.1.call-update) | async-done | bytes 2097168 | tf_op jit(solution)/shard_map/all_gather | solution.py:27
  41.4 7.1 %gather_fusion = bf16[64,128,512]{2,1,0:T(8,128)(2,1)} fusion(bf16[16,128,512]{2,1,0:T(8,128)(2,1)} %bitcast.77, s32[1024]{0:T(1024)S(1)} %pad_clamp_fusion), kind=kCustom, calls=%fused_computation | custom fusion | bytes 16777472 | tf_op jit(solution)/shard_map/gather | solution.py:28
  48.6 0.0 copy-start.3
  48.6 0.0 copy-done
  48.6 7.1 %fusion.12 = bf16[8,128,512]{1,2,0:T(8,128)(2,1)} fusion(bf16[8,8,128,512]{3,2,1,0:T(8,128)(2,1)} %bitcast.81, bf16[8,1,8,128,128]{4,3,2,1,0:T(8,128)(2,1)S(1)} %copy-done), kind=kOutput, calls=%fused_computation.12 | convolution fusion | flops 1074266112 | bytes 11534336 | tf_op jit(solution)/shard_map/rsij,rsjm->rim/dot_general | solution.py:29
  55.7 0.0 reduce-scatter.4.cloned.1.call-update
  55.7 0.0 all-gather.6.cloned.1.call-start
  55.8 0.0 copy-done.3
  55.8 0.1 fusion.28
  55.9 27.2 %reduce-scatter.4.cloned.1.call-done = bf16[2,128,512]{1,2,0:T(8,128)(2,1)} async-done(((bf16[8,128,512]{1,2,0:T(8,128)(2,1)}), bf16[2,128,512]{1,2,0:T(8,128)(2,1)}) %reduce-scatter.4.cloned.1.call-update) | async-done | bytes 262160 | tf_op jit(solution)/shard_map/reduce_scatter | solution.py:30
  83.1 1.1 copy.16
  84.2 0.1 mul.56
  84.3 0.8 fusion.21
  85.1 0.0 all-gather.6.cloned.1.call-update
  85.2 0.0 reduce-scatter.6.cloned.1.call-start
  85.2 29.3 %all-gather.6.cloned.1.call-done = bf16[2048,512]{1,0:T(8,128)(2,1)} async-done(((bf16[256,512]{1,0:T(8,128)(2,1)}), bf16[2048,512]{1,0:T(8,128)(2,1)}) %all-gather.6.cloned.1.call-update) | async-done | bytes 2097168 | tf_op jit(solution)/shard_map/all_gather | solution.py:27
  114.5 7.1 %gather_fusion.1 = bf16[64,128,512]{2,1,0:T(8,128)(2,1)} fusion(bf16[16,128,512]{2,1,0:T(8,128)(2,1)} %bitcast.79, s32[1024]{0:T(1024)S(1)} %pad_clamp_fusion), kind=kCustom, calls=%fused_computation.1 | custom fusion | bytes 16777472 | tf_op jit(solution)/shard_map/gather | solution.py:28
  121.6 0.0 copy-start.2
  121.6 7.1 %fusion.15 = bf16[8,128,512]{1,2,0:T(8,128)(2,1)} fusion(bf16[8,8,128,512]{3,2,1,0:T(8,128)(2,1)} %bitcast.82, bf16[8,1,8,128,128]{4,3,2,1,0:T(8,128)(2,1)S(1)} %copy-done), kind=kOutput, calls=%fused_computation.13 | convolution fusion | flops 1074266112 | bytes 11534336 | tf_op jit(solution)/shard_map/rsij,rsjm->rim/dot_general | solution.py:29
  128.8 0.0 reduce-scatter.6.cloned.1.call-update
  128.8 0.0 all-gather.8.cloned.1.call-start
  128.8 27.3 %reduce-scatter.6.cloned.1.call-done = bf16[2,128,512]{1,2,0:T(8,128)(2,1)} async-done(((bf16[8,128,512]{1,2,0:T(8,128)(2,1)}), bf16[2,128,512]{1,2,0:T(8,128)(2,1)}) %reduce-scatter.6.cloned.1.call-update) | async-done | bytes 262160 | tf_op jit(solution)/shard_map/reduce_scatter | solution.py:30
  156.2 1.8 convert_multiply_fusion.1
  157.9 1.2 copy.18
  159.2 0.0 copy-done.2
  159.2 0.8 fusion.22
  160.0 0.0 all-gather.8.cloned.1.call-update
  160.0 0.2 reduce-scatter.8.cloned.1.call-start
  160.3 29.0 %all-gather.8.cloned.1.call-done = bf16[2048,512]{1,0:T(8,128)(2,1)} async-done(((bf16[256,512]{1,0:T(8,128)(2,1)}), bf16[2048,512]{1,0:T(8,128)(2,1)}) %all-gather.8.cloned.1.call-update) | async-done | bytes 2097168 | tf_op jit(solution)/shard_map/all_gather | solution.py:27
  189.3 7.1 %gather_fusion.2 = bf16[64,128,512]{2,1,0:T(8,128)(2,1)} fusion(bf16[16,128,512]{2,1,0:T(8,128)(2,1)} %bitcast.78, s32[1024]{0:T(1024)S(1)} %pad_clamp_fusion), kind=kCustom, calls=%fused_computation.2 | custom fusion | bytes 16777472 | tf_op jit(solution)/shard_map/gather | solution.py:28
  196.4 0.0 copy-start.1
  196.4 7.1 %fusion.18 = bf16[8,128,512]{1,2,0:T(8,128)(2,1)} fusion(bf16[8,8,128,512]{3,2,1,0:T(8,128)(2,1)} %bitcast.80, bf16[8,1,8,128,128]{4,3,2,1,0:T(8,128)(2,1)S(1)} %copy-done), kind=kOutput, calls=%fused_computation.14 | convolution fusion | flops 1074266112 | bytes 11534336 | tf_op jit(solution)/shard_map/rsij,rsjm->rim/dot_general | solution.py:29
  203.6 0.0 reduce-scatter.8.cloned.1.call-update
  203.6 27.4 %reduce-scatter.8.cloned.1.call-done = bf16[2,128,512]{1,2,0:T(8,128)(2,1)} async-done(((bf16[8,128,512]{1,2,0:T(8,128)(2,1)}), bf16[2,128,512]{1,2,0:T(8,128)(2,1)}) %reduce-scatter.8.cloned.1.call-update) | async-done | bytes 262160 | tf_op jit(solution)/shard_map/reduce_scatter | solution.py:30
  231.0 1.8 convert_multiply_fusion
  232.8 1.2 copy.20
  234.0 0.0 copy-done.1
  234.0 0.8 fusion.23
  (2 shorter events, 0.0 us)
Async XLA Ops:
  7.2 41.4 %copy-start = (bf16[8,1,8,128,128]{4,3,2,1,0:T(8,128)(2,1)S(1)}, bf16[8,1,8,128,128]{4,3,2,1,0:T(8,128)(2,1)}, u32[]{:S(2)}) copy-start(bf16[8,1,8,128,128]{4,3,2,1,0:T(8,128)(2,1)} %param.5) | copy-start | bytes 6291460
  7.2 34.3 %all-gather.4.cloned.1.call-start = ((), (), s32[]{:S(2)}) async-start(), calls=%async_computation.3 | async-start | bytes 2359296 | tf_op jit(solution)/shard_map/all_gather | solution.py:27
  7.9 75.2 %reduce-scatter.4.cloned.1.call-start = ((), (), s32[]{:S(2)}) async-start(), calls=%async_computation.4 | async-start | bytes 1310720 | tf_op jit(solution)/shard_map/reduce_scatter | solution.py:30
  48.6 7.2 %copy-start.3 = (s32[2,3]{1,0:T(2,128)S(1)}, s32[2,3]{1,0:T(2,128)}, u32[]{:S(2)}) copy-start(s32[2,3]{1,0:T(2,128)} %param.7) | copy-start | bytes 76
  55.7 58.8 %all-gather.6.cloned.1.call-start = ((), (), s32[]{:S(2)}) async-start(), calls=%async_computation.5 | async-start | bytes 2359296 | tf_op jit(solution)/shard_map/all_gather | solution.py:27
  85.2 71.0 %reduce-scatter.6.cloned.1.call-start = ((), (), s32[]{:S(2)}) async-start(), calls=%async_computation.6 | async-start | bytes 1310720 | tf_op jit(solution)/shard_map/reduce_scatter | solution.py:30
  121.6 37.6 %copy-start.2 = (bf16[256,512]{1,0:T(8,128)(2,1)S(1)}, bf16[256,512]{1,0:T(8,128)(2,1)}, u32[]{:S(2)}) copy-start(bf16[256,512]{1,0:T(8,128)(2,1)} %param.4) | copy-start | bytes 786436
  128.8 60.5 %all-gather.8.cloned.1.call-start = ((), (), s32[]{:S(2)}) async-start(), calls=%async_computation.7 | async-start | bytes 2359296 | tf_op jit(solution)/shard_map/all_gather | solution.py:27
  160.0 70.9 %reduce-scatter.8.cloned.1.call-start = ((), (), s32[]{:S(2)}) async-start(), calls=%async_computation.8 | async-start | bytes 1310720 | tf_op jit(solution)/shard_map/reduce_scatter | solution.py:30
  196.4 37.6 %copy-start.1 = (bf16[256,512]{1,0:T(8,128)(2,1)S(1)}, bf16[256,512]{1,0:T(8,128)(2,1)}, u32[]{:S(2)}) copy-start(bf16[256,512]{1,0:T(8,128)(2,1)} %fusion.21) | copy-start | bytes 786436
Sparse Core Ops, SparseCore 0:
  9.6 31.7 all-gather.3
  55.8 27.2 reduce-scatter.3
  85.4 29.0 all-gather.5
  128.9 27.2 reduce-scatter.5
  160.2 29.0 all-gather.7
  203.7 27.2 reduce-scatter.7
where the time goes:
time: 242 us
  waiting for transfers between devices  174 us (72%)
  local copies, waits for them, and re-layouts  25.2 us (10%)
  matrix products  21.4 us (9%)
  between operations  14.2 us (6%)
  other arithmetic  6.82 us (3%)
    all_gather x3, waiting for transfers between devices, apply_slab(): lax.all_gather(slab, 'row', axis=0, tiled=True).reshape(-1, BS, width)  91 us
    reduce_scatter x3, waiting for transfers between devices, apply_slab(): lax.psum_scatter(result.astype(jnp.bfloat16).astype(jnp.float32).astype(j...  81.9 us
    dot_general x3, matrix products, apply_slab(): jnp.einsum('rsij,rsjm->rim', blocks, picked, preferred_element_type=jnp.f...  21.4 us
    gather x3, local copies, waits for them, and re-layouts, apply_slab(): picked = gathered[local_index]  21.4 us
  transfers between devices with their start and end apart: 6, of which 6 were waited for; matrix products, arithmetic and copies ran while one was open for 0% of the time, Pallas kernels for 0%

commit v1 on v0

--- a/solution.py
+++ b/solution.py
@@ -5,6 +5,27 @@
 
 BS = 128
 STEPS = 3
+
+
+def collect(value, axis, dim):
+    size, position, rows = (lax.axis_size(axis), lax.axis_index(axis), value.shape[dim])
+    right = [(i, (i + 1) % size) for i in range(size)]
+    backward = [(i, (i - 1) % size) for i in range(size)]
+    result = jnp.zeros((*value.shape[:dim], size * rows, *value.shape[dim + 1 :]), value.dtype)
+    result = lax.dynamic_update_slice_in_dim(result, value, position * rows, axis=dim)
+    from_left = from_right = value
+    middle = size // 2
+    for hop in range(1, middle + 1):
+        from_left = lax.ppermute(from_left, axis, right)
+        result = lax.dynamic_update_slice_in_dim(
+            result, from_left, (position - hop) % size * rows, axis=dim
+        )
+        if hop < size - middle:
+            from_right = lax.ppermute(from_right, axis, backward)
+            result = lax.dynamic_update_slice_in_dim(
+                result, from_right, (position + hop) % size * rows, axis=dim
+            )
+    return result
 
 
 def per_device(t_start, h_blocks, h_cols, t_cols):
@@ -24,7 +45,7 @@
         return shaped.reshape(rows_here * BS, width)
 
     def apply_slab(slab):
-        gathered = lax.all_gather(slab, "row", axis=0, tiled=True).reshape(-1, BS, width)
+        gathered = collect(slab, "row", 0).reshape(-1, BS, width)
         picked = gathered[local_index]
         result = jnp.einsum("rsij,rsjm->rim", blocks, picked, preferred_element_type=jnp.float32)
         summed = lax.psum_scatter(

time: 242 us -> 254 us (1.050)
  waiting for transfers between devices: 174 us -> 133 us
  starting transfers between devices: 0.42 us -> 32.7 us
  local copies, waits for them, and re-layouts: 25.2 us -> 46.3 us
    all_gather x3 -> x0, waiting for transfers between devices: 91 us -> none  [apply_slab(): lax.all_gather(slab, 'row', axis=0, tiled=True).reshape(-1, BS, width)]
    ppermute x0 -> x21, waiting for transfers between devices: none -> 55.5 us  [the longest x12 49.9 us: collect(): from_left = lax.ppermute(from_left, axis, right)]
    ppermute x0 -> x21, starting transfers between devices: none -> 32.6 us  [the longest x9 32 us: collect(): from_right = lax.ppermute(from_right, axis, backward)]
    dynamic_update_slice x0 -> x22, local copies, waits for them, and re-layouts: none -> 16 us  [the longest x12 8.69 us: collect(): lax.dynamic_update_slice_in_dim(result, from_left, (position - hop) % siz...]
    another operation x0 -> x3, local copies, waits for them, and re-layouts: none -> 4.59 us
    reduce_scatter x3, waiting for transfers between devices: 81.9 us -> 77.6 us  [apply_slab(): lax.psum_scatter(result.astype(jnp.bfloat16).astype(jnp.float32).astype(j...]
  transfers between devices with their start and end apart: 6 -> 24, of which waited for: 6 -> 16; matrix products, arithmetic and copies ran while one was open for 0% -> 6% of each run, Pallas kernels for 0% -> 0%
where the time goes in v1:
time: 254 us; the launch traced here: 253 us
  waiting for transfers between devices  133 us (52%)
  local copies, waits for them, and re-layouts  46.3 us (18%)
  starting transfers between devices  32.7 us (13%)
  matrix products  21.3 us (8%)
  between operations  13.9 us (5%)
  other arithmetic  6.1 us (2%)
    reduce_scatter x3, waiting for transfers between devices, apply_slab(): lax.psum_scatter(result.astype(jnp.bfloat16).astype(jnp.float32).astype(j...  77.6 us
    ppermute x12, waiting for transfers between devices, collect(): from_left = lax.ppermute(from_left, axis, right)  49.9 us
    ppermute x9, starting transfers between devices, collect(): from_right = lax.ppermute(from_right, axis, backward)  32 us
    gather x3, local copies, waits for them, and re-layouts, apply_slab(): picked = gathered[local_index]  21.5 us
    dot_general x3, matrix products, apply_slab(): jnp.einsum('rsij,rsjm->rim', blocks, picked, preferred_element_type=jnp.f...  21.3 us
    dynamic_update_slice x12, local copies, waits for them, and re-layouts, collect(): lax.dynamic_update_slice_in_dim(result, from_left, (position - hop) % siz...  8.69 us
    dynamic_update_slice x9, local copies, waits for them, and re-layouts, collect(): lax.dynamic_update_slice_in_dim(result, from_right, (position + hop) % si...  6.54 us
    ppermute x9, waiting for transfers between devices, collect(): from_right = lax.ppermute(from_right, axis, backward)  5.58 us
  transfers between devices with their start and end apart: 24, of which 16 were waited for; matrix products, arithmetic and copies ran while one was open for 6% of the time, Pallas kernels for 0%

profile of v1, /device:TPU:0, one launch (start us, length us, event | category | flops | bytes accessed | tf_op | source)
XLA Modules:
  0.0 253.5 jit_solution(11444041501464159267)
XLA Ops:
  7.7 4.1 %collective-permute-start.1 = (bf16[256,512]{1,0:T(8,128)(2,1)}, bf16[256,512]{1,0:T(8,128)(2,1)S(1)}, u32[]{:S(2)}, u32[]{:S(2)}) collective-permute-start(bf16[256,512]{1,0:T(8,128)(2,1)} %param.4), channel_id=1, source_target_pairs={{0,7},{1,0},{2,1},{3,2},{4,3},{5,4},{6,5},{7,6},{8,15},{9,8},{10,9... | collective-permute-start | bytes 786440 | tf_op jit(solution)/shard_map/ppermute | solution.py:24
  11.8 4.4 %collective-permute-done = bf16[256,512]{1,0:T(8,128)(2,1)S(1)} collective-permute-done((bf16[256,512]{1,0:T(8,128)(2,1)}, bf16[256,512]{1,0:T(8,128)(2,1)S(1)}, u32[]{:S(2)}, u32[]{:S(2)}) %collective-permute-start) | collective-permute-done | bytes 262176 | tf_op jit(solution)/shard_map/ppermute | solution.py:19
  17.0 1.5 broadcast.134.clone.1
  18.5 0.7 constant_dynamic-update-slice_fusion.23
  19.3 3.5 %collective-permute-start.3 = (bf16[256,512]{1,0:T(8,128)(2,1)S(1)}, bf16[256,512]{1,0:T(8,128)(2,1)S(1)}, u32[]{:S(2)}, u32[]{:S(2)}) collective-permute-start(bf16[256,512]{1,0:T(8,128)(2,1)S(1)} %collective-permute-done.1), channel_id=1, source_target_pairs={{0,7},{1,0},{2,1},{3,2},{4,3},{5,4},{6,5},{7,6},{8,15},{9,8},{10,9... | collective-permute-start | bytes 786440 | tf_op jit(solution)/shard_map/ppermute | solution.py:24
  22.8 1.0 collective-permute-done.2
  23.9 0.7 constant_dynamic-update-slice_fusion.22
  24.6 0.7 constant_dynamic-update-slice_fusion.21
  25.3 3.5 %collective-permute-done.3 = bf16[256,512]{1,0:T(8,128)(2,1)S(1)} collective-permute-done((bf16[256,512]{1,0:T(8,128)(2,1)S(1)}, bf16[256,512]{1,0:T(8,128)(2,1)S(1)}, u32[]{:S(2)}, u32[]{:S(2)}) %collective-permute-start.3) | collective-permute-done | bytes 262176 | tf_op jit(solution)/shard_map/ppermute | solution.py:24
  28.9 3.9 %collective-permute-start.5 = (bf16[256,512]{1,0:T(8,128)(2,1)S(1)}, bf16[256,512]{1,0:T(8,128)(2,1)S(1)}, u32[]{:S(2)}, u32[]{:S(2)}) collective-permute-start(bf16[256,512]{1,0:T(8,128)(2,1)S(1)} %collective-permute-done.3), channel_id=1, source_target_pairs={{0,7},{1,0},{2,1},{3,2},{4,3},{5,4},{6,5},{7,6},{8,15},{9,8},{10,9... | collective-permute-start | bytes 786440 | tf_op jit(solution)/shard_map/ppermute | solution.py:24
  34.9 2.0 collective-permute-done.5
  37.7 3.4 %collective-permute-done.6 = bf16[256,512]{1,0:T(8,128)(2,1)S(1)} collective-permute-done((bf16[256,512]{1,0:T(8,128)(2,1)S(1)}, bf16[256,512]{1,0:T(8,128)(2,1)S(1)}, u32[]{:S(2)}, u32[]{:S(2)}) %collective-permute-start.6) | collective-permute-done | bytes 262176 | tf_op jit(solution)/shard_map/ppermute | solution.py:19
  41.8 7.2 %gather_fusion = bf16[64,128,512]{2,1,0:T(8,128)(2,1)} fusion(bf16[16,128,512]{2,1,0:T(8,128)(2,1)} %bitcast, s32[1024]{0:T(1024)S(1)} %pad_clamp_fusion), kind=kCustom, calls=%fused_computation | custom fusion | bytes 16777472 | tf_op jit(solution)/shard_map/gather | solution.py:49
  49.0 7.1 %fusion.12 = bf16[8,128,512]{1,2,0:T(8,128)(2,1)} fusion(bf16[8,8,128,512]{3,2,1,0:T(8,128)(2,1)} %bitcast.75, bf16[8,1,8,128,128]{4,3,2,1,0:T(8,128)(2,1)S(1)} %copy-done), kind=kOutput, calls=%fused_computation.12 | convolution fusion | flops 1074266112 | bytes 11534336 | tf_op jit(solution)/shard_map/rsij,rsjm->rim/dot_general | solution.py:50
  56.3 27.6 %reduce-scatter.4.cloned.1.call-done = bf16[2,128,512]{1,2,0:T(8,128)(2,1)} async-done(((bf16[8,128,512]{1,2,0:T(8,128)(2,1)}), bf16[2,128,512]{1,2,0:T(8,128)(2,1)}) %reduce-scatter.4.cloned.1.call-update) | async-done | bytes 262160 | tf_op jit(solution)/shard_map/reduce_scatter | solution.py:51
  83.8 1.1 copy.13
  85.0 1.5 broadcast.134.clone
  86.6 0.8 constant_dynamic-update-slice_fusion.15
  88.1 2.8 %collective-permute-start.8 = (bf16[256,512]{1,0:T(8,128)(2,1)S(1)}, bf16[256,512]{1,0:T(8,128)(2,1)S(1)}, u32[]{:S(2)}, u32[]{:S(2)}) collective-permute-start(bf16[256,512]{1,0:T(8,128)(2,1)S(1)} %get-tuple-element.3), channel_id=1, source_target_pairs={{0,7},{1,0},{2,1},{3,2},{4,3},{5,4},{6,5},{7,6},{8,15},{9,8},{10,9... | collective-permute-start | bytes 786440 | tf_op jit(solution)/shard_map/ppermute | solution.py:24
  90.9 5.0 %collective-permute-done.7 = bf16[256,512]{1,0:T(8,128)(2,1)S(1)} collective-permute-done((bf16[256,512]{1,0:T(8,128)(2,1)S(1)}, bf16[256,512]{1,0:T(8,128)(2,1)S(1)}, u32[]{:S(2)}, u32[]{:S(2)}) %collective-permute-start.7) | collective-permute-done | bytes 262176 | tf_op jit(solution)/shard_map/ppermute | solution.py:19
  95.9 3.5 %collective-permute-start.10 = (bf16[256,512]{1,0:T(8,128)(2,1)S(1)}, bf16[256,512]{1,0:T(8,128)(2,1)S(1)}, u32[]{:S(2)}, u32[]{:S(2)}) collective-permute-start(bf16[256,512]{1,0:T(8,128)(2,1)S(1)} %collective-permute-done.8), channel_id=1, source_target_pairs={{0,7},{1,0},{2,1},{3,2},{4,3},{5,4},{6,5},{7,6},{8,15},{9,8},{10,9... | collective-permute-start | bytes 786440 | tf_op jit(solution)/shard_map/ppermute | solution.py:24
  99.5 6.8 %collective-permute-done.9 = bf16[256,512]{1,0:T(8,128)(2,1)S(1)} collective-permute-done((bf16[256,512]{1,0:T(8,128)(2,1)S(1)}, bf16[256,512]{1,0:T(8,128)(2,1)S(1)}, u32[]{:S(2)}, u32[]{:S(2)}) %collective-permute-start.9) | collective-permute-done | bytes 262176 | tf_op jit(solution)/shard_map/ppermute | solution.py:19
  106.2 0.7 constant_dynamic-update-slice_fusion.14
  107.0 0.7 constant_dynamic-update-slice_fusion.13
  107.7 3.5 %collective-permute-start.12 = (bf16[256,512]{1,0:T(8,128)(2,1)S(1)}, bf16[256,512]{1,0:T(8,128)(2,1)S(1)}, u32[]{:S(2)}, u32[]{:S(2)}) collective-permute-start(bf16[256,512]{1,0:T(8,128)(2,1)S(1)} %collective-permute-done.10), channel_id=1, source_target_pairs={{0,7},{1,0},{2,1},{3,2},{4,3},{5,4},{6,5},{7,6},{8,15},{9,8},{10,9... | collective-permute-start | bytes 786440 | tf_op jit(solution)/shard_map/ppermute | solution.py:24
  112.0 3.4 %collective-permute-done.11 = bf16[256,512]{1,0:T(8,128)(2,1)S(1)} collective-permute-done((bf16[256,512]{1,0:T(8,128)(2,1)S(1)}, bf16[256,512]{1,0:T(8,128)(2,1)S(1)}, u32[]{:S(2)}, u32[]{:S(2)}) %collective-permute-start.11) | collective-permute-done | bytes 262176 | tf_op jit(solution)/shard_map/ppermute | solution.py:19
  117.5 5.4 %collective-permute-done.13 = bf16[256,512]{1,0:T(8,128)(2,1)S(1)} collective-permute-done((bf16[256,512]{1,0:T(8,128)(2,1)S(1)}, bf16[256,512]{1,0:T(8,128)(2,1)S(1)}, u32[]{:S(2)}, u32[]{:S(2)}) %collective-permute-start.13) | collective-permute-done | bytes 262176 | tf_op jit(solution)/shard_map/ppermute | solution.py:19
  123.6 7.2 %gather_fusion.1 = bf16[64,128,512]{2,1,0:T(8,128)(2,1)} fusion(bf16[16,128,512]{2,1,0:T(8,128)(2,1)} %bitcast.8, s32[1024]{0:T(1024)S(1)} %pad_clamp_fusion), kind=kCustom, calls=%fused_computation.1 | custom fusion | bytes 16777472 | tf_op jit(solution)/shard_map/gather | solution.py:49
  130.8 7.1 %fusion.15 = bf16[8,128,512]{1,2,0:T(8,128)(2,1)} fusion(bf16[8,8,128,512]{3,2,1,0:T(8,128)(2,1)} %bitcast.76, bf16[8,1,8,128,128]{4,3,2,1,0:T(8,128)(2,1)S(1)} %copy-done), kind=kOutput, calls=%fused_computation.13 | convolution fusion | flops 1074266112 | bytes 11534336 | tf_op jit(solution)/shard_map/rsij,rsjm->rim/dot_general | solution.py:50
  138.0 25.0 %reduce-scatter.6.cloned.1.call-done = bf16[2,128,512]{1,2,0:T(8,128)(2,1)} async-done(((bf16[8,128,512]{1,2,0:T(8,128)(2,1)}), bf16[2,128,512]{1,2,0:T(8,128)(2,1)}) %reduce-scatter.6.cloned.1.call-update) | async-done | bytes 262160 | tf_op jit(solution)/shard_map/reduce_scatter | solution.py:51
  163.0 1.0 convert_multiply_fusion.1
  164.0 1.0 copy.15
  165.0 1.5 broadcast.134
  166.6 0.9 constant_dynamic-update-slice_fusion.7
  167.4 3.5 %collective-permute-start.15 = (bf16[256,512]{1,0:T(8,128)(2,1)S(1)}, bf16[256,512]{1,0:T(8,128)(2,1)S(1)}, u32[]{:S(2)}, u32[]{:S(2)}) collective-permute-start(bf16[256,512]{1,0:T(8,128)(2,1)S(1)} %get-tuple-element.5), channel_id=1, source_target_pairs={{0,7},{1,0},{2,1},{3,2},{4,3},{5,4},{6,5},{7,6},{8,15},{9,8},{10,9... | collective-permute-start | bytes 786440 | tf_op jit(solution)/shard_map/ppermute | solution.py:24
  171.0 5.0 %collective-permute-done.14 = bf16[256,512]{1,0:T(8,128)(2,1)S(1)} collective-permute-done((bf16[256,512]{1,0:T(8,128)(2,1)S(1)}, bf16[256,512]{1,0:T(8,128)(2,1)S(1)}, u32[]{:S(2)}, u32[]{:S(2)}) %collective-permute-start.14) | collective-permute-done | bytes 262176 | tf_op jit(solution)/shard_map/ppermute | solution.py:19
  176.0 3.5 %collective-permute-start.17 = (bf16[256,512]{1,0:T(8,128)(2,1)S(1)}, bf16[256,512]{1,0:T(8,128)(2,1)S(1)}, u32[]{:S(2)}, u32[]{:S(2)}) collective-permute-start(bf16[256,512]{1,0:T(8,128)(2,1)S(1)} %collective-permute-done.15), channel_id=1, source_target_pairs={{0,7},{1,0},{2,1},{3,2},{4,3},{5,4},{6,5},{7,6},{8,15},{9,8},{10,9... | collective-permute-start | bytes 786440 | tf_op jit(solution)/shard_map/ppermute | solution.py:24
  179.5 6.8 %collective-permute-done.16 = bf16[256,512]{1,0:T(8,128)(2,1)S(1)} collective-permute-done((bf16[256,512]{1,0:T(8,128)(2,1)S(1)}, bf16[256,512]{1,0:T(8,128)(2,1)S(1)}, u32[]{:S(2)}, u32[]{:S(2)}) %collective-permute-start.16) | collective-permute-done | bytes 262176 | tf_op jit(solution)/shard_map/ppermute | solution.py:19
  187.1 0.7 constant_dynamic-update-slice_fusion.5
  187.8 3.5 %collective-permute-start.19 = (bf16[256,512]{1,0:T(8,128)(2,1)S(1)}, bf16[256,512]{1,0:T(8,128)(2,1)S(1)}, u32[]{:S(2)}, u32[]{:S(2)}) collective-permute-start(bf16[256,512]{1,0:T(8,128)(2,1)S(1)} %collective-permute-done.17), channel_id=1, source_target_pairs={{0,7},{1,0},{2,1},{3,2},{4,3},{5,4},{6,5},{7,6},{8,15},{9,8},{10,9... | collective-permute-start | bytes 786440 | tf_op jit(solution)/shard_map/ppermute | solution.py:24
  192.1 3.3 %collective-permute-done.18 = bf16[256,512]{1,0:T(8,128)(2,1)S(1)} collective-permute-done((bf16[256,512]{1,0:T(8,128)(2,1)S(1)}, bf16[256,512]{1,0:T(8,128)(2,1)S(1)}, u32[]{:S(2)}, u32[]{:S(2)}) %collective-permute-start.18) | collective-permute-done | bytes 262176 | tf_op jit(solution)/shard_map/ppermute | solution.py:19
  197.6 5.4 %collective-permute-done.20 = bf16[256,512]{1,0:T(8,128)(2,1)S(1)} collective-permute-done((bf16[256,512]{1,0:T(8,128)(2,1)S(1)}, bf16[256,512]{1,0:T(8,128)(2,1)S(1)}, u32[]{:S(2)}, u32[]{:S(2)}) %collective-permute-start.20) | collective-permute-done | bytes 262176 | tf_op jit(solution)/shard_map/ppermute | solution.py:19
  203.7 7.2 %gather_fusion.2 = bf16[64,128,512]{2,1,0:T(8,128)(2,1)} fusion(bf16[16,128,512]{2,1,0:T(8,128)(2,1)} %bitcast.14, s32[1024]{0:T(1024)S(1)} %pad_clamp_fusion), kind=kCustom, calls=%fused_computation.2 | custom fusion | bytes 16777472 | tf_op jit(solution)/shard_map/gather | solution.py:49
  210.9 7.1 %fusion.18 = bf16[8,128,512]{1,2,0:T(8,128)(2,1)} fusion(bf16[8,8,128,512]{3,2,1,0:T(8,128)(2,1)} %bitcast.74, bf16[8,1,8,128,128]{4,3,2,1,0:T(8,128)(2,1)S(1)} %copy-done), kind=kOutput, calls=%fused_computation.14 | convolution fusion | flops 1074266112 | bytes 11534336 | tf_op jit(solution)/shard_map/rsij,rsjm->rim/dot_general | solution.py:50
  218.0 25.1 %reduce-scatter.8.cloned.1.call-done = bf16[2,128,512]{1,2,0:T(8,128)(2,1)} async-done(((bf16[8,128,512]{1,2,0:T(8,128)(2,1)}), bf16[2,128,512]{1,2,0:T(8,128)(2,1)}) %reduce-scatter.8.cloned.1.call-update) | async-done | bytes 262160 | tf_op jit(solution)/shard_map/reduce_scatter | solution.py:51
  243.1 1.8 convert_multiply_fusion
  244.9 1.2 copy.17
  246.1 0.8 fusion.23
  (62 shorter events, 14.0 us)
Async XLA Ops:
  7.2 41.8 %copy-start = (bf16[8,1,8,128,128]{4,3,2,1,0:T(8,128)(2,1)S(1)}, bf16[8,1,8,128,128]{4,3,2,1,0:T(8,128)(2,1)}, u32[]{:S(2)}) copy-start(bf16[8,1,8,128,128]{4,3,2,1,0:T(8,128)(2,1)} %param.5) | copy-start | bytes 6291460
  7.2 11.4 %copy-start.2 = (bf16[256,512]{1,0:T(8,128)(2,1)S(1)}, bf16[256,512]{1,0:T(8,128)(2,1)}, u32[]{:S(2)}) copy-start(bf16[256,512]{1,0:T(8,128)(2,1)} %param.4) | copy-start | bytes 786436
  7.2 76.6 %reduce-scatter.4.cloned.1.call-start = ((), (), s32[]{:S(2)}) async-start(), calls=%async_computation.3 | async-start | bytes 1310720 | tf_op jit(solution)/shard_map/reduce_scatter | solution.py:51
  7.2 9.0 %collective-permute-start = (bf16[256,512]{1,0:T(8,128)(2,1)}, bf16[256,512]{1,0:T(8,128)(2,1)S(1)}, u32[]{:S(2)}, u32[]{:S(2)}) collective-permute-start(bf16[256,512]{1,0:T(8,128)(2,1)} %param.4), channel_id=1, source_target_pairs={{0,1},{1,2},{2,3},{3,4},{4,5},{5,6},{6,7},{7,0},{8,9},{9,10},{10,1... | collective-permute-start | bytes 786440 | tf_op jit(solution)/shard_map/ppermute | solution.py:19
  7.7 11.5 %collective-permute-start.1 = (bf16[256,512]{1,0:T(8,128)(2,1)}, bf16[256,512]{1,0:T(8,128)(2,1)S(1)}, u32[]{:S(2)}, u32[]{:S(2)}) collective-permute-start(bf16[256,512]{1,0:T(8,128)(2,1)} %param.4), channel_id=1, source_target_pairs={{0,7},{1,0},{2,1},{3,2},{4,3},{5,4},{6,5},{7,6},{8,15},{9,8},{10,9... | collective-permute-start | bytes 786440 | tf_op jit(solution)/shard_map/ppermute | solution.py:24
  16.2 7.7 %collective-permute-start.2 = (bf16[256,512]{1,0:T(8,128)(2,1)S(1)}, bf16[256,512]{1,0:T(8,128)(2,1)S(1)}, u32[]{:S(2)}, u32[]{:S(2)}) collective-permute-start(bf16[256,512]{1,0:T(8,128)(2,1)S(1)} %collective-permute-done), channel_id=1, source_target_pairs={{0,1},{1,2},{2,3},{3,4},{4,5},{5,6},{6,7},{7,0},{8,9},{9,10},{10,1... | collective-permute-start | bytes 786440 | tf_op jit(solution)/shard_map/ppermute | solution.py:19
  19.3 9.6 %collective-permute-start.3 = (bf16[256,512]{1,0:T(8,128)(2,1)S(1)}, bf16[256,512]{1,0:T(8,128)(2,1)S(1)}, u32[]{:S(2)}, u32[]{:S(2)}) collective-permute-start(bf16[256,512]{1,0:T(8,128)(2,1)S(1)} %collective-permute-done.1), channel_id=1, source_target_pairs={{0,7},{1,0},{2,1},{3,2},{4,3},{5,4},{6,5},{7,6},{8,15},{9,8},{10,9... | collective-permute-start | bytes 786440 | tf_op jit(solution)/shard_map/ppermute | solution.py:24
  23.9 9.6 %collective-permute-start.4 = (bf16[256,512]{1,0:T(8,128)(2,1)S(1)}, bf16[256,512]{1,0:T(8,128)(2,1)S(1)}, u32[]{:S(2)}, u32[]{:S(2)}) collective-permute-start(bf16[256,512]{1,0:T(8,128)(2,1)S(1)} %collective-permute-done.2), channel_id=1, source_target_pairs={{0,1},{1,2},{2,3},{3,4},{4,5},{5,6},{6,7},{7,0},{8,9},{9,10},{10,1... | collective-permute-start | bytes 786440 | tf_op jit(solution)/shard_map/ppermute | solution.py:19
  28.9 8.1 %collective-permute-start.5 = (bf16[256,512]{1,0:T(8,128)(2,1)S(1)}, bf16[256,512]{1,0:T(8,128)(2,1)S(1)}, u32[]{:S(2)}, u32[]{:S(2)}) collective-permute-start(bf16[256,512]{1,0:T(8,128)(2,1)S(1)} %collective-permute-done.3), channel_id=1, source_target_pairs={{0,7},{1,0},{2,1},{3,2},{4,3},{5,4},{6,5},{7,6},{8,15},{9,8},{10,9... | collective-permute-start | bytes 786440 | tf_op jit(solution)/shard_map/ppermute | solution.py:24
  33.5 7.6 %collective-permute-start.6 = (bf16[256,512]{1,0:T(8,128)(2,1)S(1)}, bf16[256,512]{1,0:T(8,128)(2,1)S(1)}, u32[]{:S(2)}, u32[]{:S(2)}) collective-permute-start(bf16[256,512]{1,0:T(8,128)(2,1)S(1)} %collective-permute-done.4), channel_id=1, source_target_pairs={{0,1},{1,2},{2,3},{3,4},{4,5},{5,6},{6,7},{7,0},{8,9},{9,10},{10,1... | collective-permute-start | bytes 786440 | tf_op jit(solution)/shard_map/ppermute | solution.py:19
  49.0 7.2 %copy-start.6 = (s32[2,3]{1,0:T(2,128)S(1)}, s32[2,3]{1,0:T(2,128)}, u32[]{:S(2)}) copy-start(s32[2,3]{1,0:T(2,128)} %param.7) | copy-start | bytes 76
  56.1 106.9 %reduce-scatter.6.cloned.1.call-start = ((), (), s32[]{:S(2)}) async-start(), calls=%async_computation.4 | async-start | bytes 1310720 | tf_op jit(solution)/shard_map/reduce_scatter | solution.py:51
  87.4 0.7 copy-start.3
  87.4 8.5 %collective-permute-start.7 = (bf16[256,512]{1,0:T(8,128)(2,1)S(1)}, bf16[256,512]{1,0:T(8,128)(2,1)S(1)}, u32[]{:S(2)}, u32[]{:S(2)}) collective-permute-start(bf16[256,512]{1,0:T(8,128)(2,1)S(1)} %get-tuple-element.3), channel_id=1, source_target_pairs={{0,1},{1,2},{2,3},{3,4},{4,5},{5,6},{6,7},{7,0},{8,9},{9,10},{10,1... | collective-permute-start | bytes 786440 | tf_op jit(solution)/shard_map/ppermute | solution.py:19
  88.1 7.8 %collective-permute-start.8 = (bf16[256,512]{1,0:T(8,128)(2,1)S(1)}, bf16[256,512]{1,0:T(8,128)(2,1)S(1)}, u32[]{:S(2)}, u32[]{:S(2)}) collective-permute-start(bf16[256,512]{1,0:T(8,128)(2,1)S(1)} %get-tuple-element.3), channel_id=1, source_target_pairs={{0,7},{1,0},{2,1},{3,2},{4,3},{5,4},{6,5},{7,6},{8,15},{9,8},{10,9... | collective-permute-start | bytes 786440 | tf_op jit(solution)/shard_map/ppermute | solution.py:24
  95.9 10.3 %collective-permute-start.9 = (bf16[256,512]{1,0:T(8,128)(2,1)S(1)}, bf16[256,512]{1,0:T(8,128)(2,1)S(1)}, u32[]{:S(2)}, u32[]{:S(2)}) collective-permute-start(bf16[256,512]{1,0:T(8,128)(2,1)S(1)} %collective-permute-done.7), channel_id=1, source_target_pairs={{0,1},{1,2},{2,3},{3,4},{4,5},{5,6},{6,7},{7,0},{8,9},{9,10},{10,1... | collective-permute-start | bytes 786440 | tf_op jit(solution)/shard_map/ppermute | solution.py:19
  95.9 11.8 %collective-permute-start.10 = (bf16[256,512]{1,0:T(8,128)(2,1)S(1)}, bf16[256,512]{1,0:T(8,128)(2,1)S(1)}, u32[]{:S(2)}, u32[]{:S(2)}) collective-permute-start(bf16[256,512]{1,0:T(8,128)(2,1)S(1)} %collective-permute-done.8), channel_id=1, source_target_pairs={{0,7},{1,0},{2,1},{3,2},{4,3},{5,4},{6,5},{7,6},{8,15},{9,8},{10,9... | collective-permute-start | bytes 786440 | tf_op jit(solution)/shard_map/ppermute | solution.py:24
  106.2 9.1 %collective-permute-start.11 = (bf16[256,512]{1,0:T(8,128)(2,1)S(1)}, bf16[256,512]{1,0:T(8,128)(2,1)S(1)}, u32[]{:S(2)}, u32[]{:S(2)}) collective-permute-start(bf16[256,512]{1,0:T(8,128)(2,1)S(1)} %collective-permute-done.9), channel_id=1, source_target_pairs={{0,1},{1,2},{2,3},{3,4},{4,5},{5,6},{6,7},{7,0},{8,9},{9,10},{10,1... | collective-permute-start | bytes 786440 | tf_op jit(solution)/shard_map/ppermute | solution.py:19
  107.7 9.1 %collective-permute-start.12 = (bf16[256,512]{1,0:T(8,128)(2,1)S(1)}, bf16[256,512]{1,0:T(8,128)(2,1)S(1)}, u32[]{:S(2)}, u32[]{:S(2)}) collective-permute-start(bf16[256,512]{1,0:T(8,128)(2,1)S(1)} %collective-permute-done.10), channel_id=1, source_target_pairs={{0,7},{1,0},{2,1},{3,2},{4,3},{5,4},{6,5},{7,6},{8,15},{9,8},{10,9... | collective-permute-start | bytes 786440 | tf_op jit(solution)/shard_map/ppermute | solution.py:24
  115.3 7.6 %collective-permute-start.13 = (bf16[256,512]{1,0:T(8,128)(2,1)S(1)}, bf16[256,512]{1,0:T(8,128)(2,1)S(1)}, u32[]{:S(2)}, u32[]{:S(2)}) collective-permute-start(bf16[256,512]{1,0:T(8,128)(2,1)S(1)} %collective-permute-done.11), channel_id=1, source_target_pairs={{0,1},{1,2},{2,3},{3,4},{4,5},{5,6},{6,7},{7,0},{8,9},{9,10},{10,1... | collective-permute-start | bytes 786440 | tf_op jit(solution)/shard_map/ppermute | solution.py:19
  137.9 105.1 %reduce-scatter.8.cloned.1.call-start = ((), (), s32[]{:S(2)}) async-start(), calls=%async_computation.5 | async-start | bytes 1310720 | tf_op jit(solution)/shard_map/reduce_scatter | solution.py:51
  165.0 1.5 copy-start.1
  167.4 43.5 %copy-start.5 = (bf16[256,512]{1,0:T(8,128)(2,1)}, bf16[256,512]{1,0:T(8,128)(2,1)S(1)}, u32[]{:S(2)}) copy-start(bf16[256,512]{1,0:T(8,128)(2,1)S(1)} %get-tuple-element.5) | copy-start | bytes 786436
  167.4 8.6 %collective-permute-start.14 = (bf16[256,512]{1,0:T(8,128)(2,1)S(1)}, bf16[256,512]{1,0:T(8,128)(2,1)S(1)}, u32[]{:S(2)}, u32[]{:S(2)}) collective-permute-start(bf16[256,512]{1,0:T(8,128)(2,1)S(1)} %get-tuple-element.5), channel_id=1, source_target_pairs={{0,1},{1,2},{2,3},{3,4},{4,5},{5,6},{6,7},{7,0},{8,9},{9,10},{10,1... | collective-permute-start | bytes 786440 | tf_op jit(solution)/shard_map/ppermute | solution.py:19
  167.4 8.6 %collective-permute-start.15 = (bf16[256,512]{1,0:T(8,128)(2,1)S(1)}, bf16[256,512]{1,0:T(8,128)(2,1)S(1)}, u32[]{:S(2)}, u32[]{:S(2)}) collective-permute-start(bf16[256,512]{1,0:T(8,128)(2,1)S(1)} %get-tuple-element.5), channel_id=1, source_target_pairs={{0,7},{1,0},{2,1},{3,2},{4,3},{5,4},{6,5},{7,6},{8,15},{9,8},{10,9... | collective-permute-start | bytes 786440 | tf_op jit(solution)/shard_map/ppermute | solution.py:24
  176.0 10.4 %collective-permute-start.16 = (bf16[256,512]{1,0:T(8,128)(2,1)S(1)}, bf16[256,512]{1,0:T(8,128)(2,1)S(1)}, u32[]{:S(2)}, u32[]{:S(2)}) collective-permute-start(bf16[256,512]{1,0:T(8,128)(2,1)S(1)} %collective-permute-done.14), channel_id=1, source_target_pairs={{0,1},{1,2},{2,3},{3,4},{4,5},{5,6},{6,7},{7,0},{8,9},{9,10},{10,1... | collective-permute-start | bytes 786440 | tf_op jit(solution)/shard_map/ppermute | solution.py:19
  176.0 11.8 %collective-permute-start.17 = (bf16[256,512]{1,0:T(8,128)(2,1)S(1)}, bf16[256,512]{1,0:T(8,128)(2,1)S(1)}, u32[]{:S(2)}, u32[]{:S(2)}) collective-permute-start(bf16[256,512]{1,0:T(8,128)(2,1)S(1)} %collective-permute-done.15), channel_id=1, source_target_pairs={{0,7},{1,0},{2,1},{3,2},{4,3},{5,4},{6,5},{7,6},{8,15},{9,8},{10,9... | collective-permute-start | bytes 786440 | tf_op jit(solution)/shard_map/ppermute | solution.py:24
  186.3 9.1 %collective-permute-start.18 = (bf16[256,512]{1,0:T(8,128)(2,1)S(1)}, bf16[256,512]{1,0:T(8,128)(2,1)S(1)}, u32[]{:S(2)}, u32[]{:S(2)}) collective-permute-start(bf16[256,512]{1,0:T(8,128)(2,1)S(1)} %collective-permute-done.16), channel_id=1, source_target_pairs={{0,1},{1,2},{2,3},{3,4},{4,5},{5,6},{6,7},{7,0},{8,9},{9,10},{10,1... | collective-permute-start | bytes 786440 | tf_op jit(solution)/shard_map/ppermute | solution.py:19
  187.8 9.0 %collective-permute-start.19 = (bf16[256,512]{1,0:T(8,128)(2,1)S(1)}, bf16[256,512]{1,0:T(8,128)(2,1)S(1)}, u32[]{:S(2)}, u32[]{:S(2)}) collective-permute-start(bf16[256,512]{1,0:T(8,128)(2,1)S(1)} %collective-permute-done.17), channel_id=1, source_target_pairs={{0,7},{1,0},{2,1},{3,2},{4,3},{5,4},{6,5},{7,6},{8,15},{9,8},{10,9... | collective-permute-start | bytes 786440 | tf_op jit(solution)/shard_map/ppermute | solution.py:24
  195.4 7.6 %collective-permute-start.20 = (bf16[256,512]{1,0:T(8,128)(2,1)S(1)}, bf16[256,512]{1,0:T(8,128)(2,1)S(1)}, u32[]{:S(2)}, u32[]{:S(2)}) collective-permute-start(bf16[256,512]{1,0:T(8,128)(2,1)S(1)} %collective-permute-done.18), channel_id=1, source_target_pairs={{0,1},{1,2},{2,3},{3,4},{4,5},{5,6},{6,7},{7,0},{8,9},{9,10},{10,1... | collective-permute-start | bytes 786440 | tf_op jit(solution)/shard_map/ppermute | solution.py:19
  218.0 28.1 %copy-start.4 = (bf16[256,512]{1,0:T(8,128)(2,1)S(1)}, bf16[256,512]{1,0:T(8,128)(2,1)}, u32[]{:S(2)}) copy-start(bf16[256,512]{1,0:T(8,128)(2,1)} %copy-done.3) | copy-start | bytes 786436
Sparse Core Ops, SparseCore 0:
  56.2 27.5 reduce-scatter.3
  138.1 24.9 reduce-scatter.5
  218.1 24.8 reduce-scatter.7
